TPU v7x, 128 devices: a whole 4x4x4 slice. The times are simulated.
128 devices in a mesh: pole: 4 (over y_lo, core), dom: 32 (over z, x, y_hi).
Axes of the slice: x: 4, y: 4 (y_hi: 2, y_lo: 2; y = y_hi * 2 + y_lo), z: 4, core: 2. Of those that a mesh axis runs over, the one named last changes fastest.
Arguments:
- initial_block: bfloat16 [32, 8, 512, 256], P('dom'), may hold values from -24 to 24
- coupling: bfloat16 [32, 8, 512, 512], P('dom'), may hold values from -0.125 to 0.125
- pivots: bfloat16 [4, 32, 8, 2, 512, 512], P('pole', 'dom'), may hold values from -0.125 to 0.125
- interface: bfloat16 [4, 32, 3, 2, 512, 512], P('pole', 'dom'), may hold values from -0.1875 to 0.1875
- pole_values: float32 [4, 4], P('pole'), may hold values from 0.5 to 1.5
Outputs:
- filtered_basis: float32 [32, 8, 512, 256], P('dom', 'pole')
- rayleigh: float32 [256, 256], replicated
All inputs are finite; a program needn't handle non-finite values.
Results may differ from a plain program's by a relative error of at most 0.008.
Values sent between devices are 32-bit elements; how exact they have to be, the bound alone decides.
A program may use at most 192 MiB of HBM per device.

v0:
```python
import jax
import jax.numpy as jnp
from jax import lax
from jax.sharding import PartitionSpec as P

B = 512
M = 256


def shifted(x, axis, by):
    length = lax.axis_size(axis)
    pairs = [(i, i + by) for i in range(length) if 0 <= i + by < length]
    return lax.ppermute(x, axis, pairs)


def lower_solve(factor, right_side):
    return lax.linalg.triangular_solve(factor, right_side, left_side=True, lower=True)


def complex_product(matrix, vectors):
    block_order = matrix.shape[1]
    half_width = vectors.shape[1] // 2
    stacked = matrix.reshape(2 * block_order, block_order)
    stacked_out = jnp.dot(stacked, vectors.astype(jnp.bfloat16), preferred_element_type=jnp.float32)
    real_part = stacked_out[:block_order, :half_width] - stacked_out[block_order:, half_width:]
    imag_part = stacked_out[:block_order, half_width:] + stacked_out[block_order:, :half_width]
    return jnp.concatenate([real_part, imag_part], axis=1)


def real_product(matrix, vectors):
    return jnp.dot(matrix, vectors.astype(jnp.bfloat16), preferred_element_type=jnp.float32)


def transposed_product(matrix, vectors):
    return lax.dot_general(
        matrix,
        vectors.astype(jnp.bfloat16),
        (((0,), (0,)), ((), ())),
        preferred_element_type=jnp.float32,
    )


def inner_products(left, right_side):
    return lax.dot_general(
        left,
        right_side,
        (((0,), (0,)), ((), ())),
        precision=lax.Precision.HIGHEST,
        preferred_element_type=jnp.float32,
    )


def partition_solve(inverse, coupled, source):
    previous = jnp.roll(coupled, 1, axis=0)
    initial = jnp.zeros(source.shape[1:], jnp.float32)

    def forward_step(carried, members):
        block_inverse, given, couple_prev = members
        result = complex_product(block_inverse, given + transposed_product(couple_prev, carried))
        return (result, result)

    unused, forward = lax.scan(forward_step, initial, (inverse, source, previous))

    def backward_step(carried, members):
        block_inverse, partial_value, couple_next = members
        result = partial_value + complex_product(block_inverse, real_product(couple_next, carried))
        return (result, result)

    unused, backward = lax.scan(backward_step, initial, (inverse, forward, coupled), reverse=True)
    return backward


def on_device(initial_block, coupling, pivots, interface, pole_values):
    blocks = coupling.shape[1]
    coupled = coupling[0]
    inverse = pivots[0, 0]
    factors = interface[0, 0]
    real_start = initial_block[0].astype(jnp.float32)
    source = jnp.concatenate([real_start, jnp.zeros_like(real_start)], axis=-1)
    first = partition_solve(inverse, coupled, source)
    bottom = first[blocks - 1]
    top = first[0]
    top_next = shifted(top, "dom", -1)
    below = complex_product(factors[0], bottom) - complex_product(factors[1], top_next)
    topmost = lax.axis_index("dom") == lax.axis_size("dom") - 1
    above = jnp.where(
        topmost, jnp.zeros_like(top_next), top_next - complex_product(factors[2], below)
    )
    link = coupled[blocks - 1]
    lifted = transposed_product(link, below)
    arriving = shifted(lifted, "dom", 1)
    update = source.at[0].add(arriving)
    update = update.at[blocks - 1].add(real_product(link, above))
    second = partition_solve(inverse, coupled, update)
    real_z = pole_values[0, 0]
    imag_z = pole_values[0, 1]
    real_w = pole_values[0, 2]
    imag_w = pole_values[0, 3]
    real_x = second[..., :M]
    imag_x = second[..., M:]
    filtered_term = real_w * real_x - imag_w * imag_x
    shifted_term = (
        (real_w * real_z - imag_w * imag_z) * real_x
        - (real_w * imag_z + imag_w * real_z) * imag_x
        - real_w * real_start
    )
    count = blocks // lax.axis_size("pole")
    owned, shifted_owned = (
        lax.psum_scatter(filtered_term[None], "pole", scatter_dimension=1, tiled=True),
        lax.psum_scatter(shifted_term[None], "pole", scatter_dimension=1, tiled=True),
    )
    own_rows = owned[0].reshape(count * B, M)
    gram_part = inner_products(own_rows, own_rows)
    projected_part = inner_products(own_rows, shifted_owned[0].reshape(count * B, M))
    gram_total, projected_total = lax.psum((gram_part, projected_part), ("pole", "dom"))
    row_total = blocks * B * lax.axis_size("dom")
    gram = gram_total / row_total
    projected = projected_total / row_total
    factor = jnp.linalg.cholesky(gram)
    filtered_basis = lower_solve(factor, own_rows.T).T.reshape(1, count, B, M)
    middle = lower_solve(factor, projected)
    rayleigh = lower_solve(factor, middle.T).T
    return (filtered_basis, rayleigh)


def solution(mesh):
    in_specs = (
        P("dom", None, None, None),
        P("dom", None, None, None),
        P("pole", "dom", None, None, None, None),
        P("pole", "dom", None, None, None, None),
        P("pole", None),
    )
    out_specs = (P("dom", "pole", None, None), P())
    return jax.shard_map(
        on_device, mesh=mesh, in_specs=in_specs, out_specs=out_specs, check_vma=False
    )
```

profile of v0, /device:TPU:1, one launch (start us, length us, event | category | flops | bytes accessed | tf_op | source)
XLA Modules:
  0.0 714.1 jit_solution(7158494593496729926)
XLA Ops:
  7.2 4.2 slice_bitcast_fusion
  12.5 2.9 copy.17
  18.0 4.2 concatenate.76
  24.6 4.3 broadcast.158.clone.2
  29.7 65.3 %while.65 = (s32[]{:T(128)}, bf16[512,512]{0,1:T(8,128)(2,1)}, f32[8,512,512]{1,2,0:T(8,128)}, bf16[8,2,512,512]{3,2,1,0:T(8,128)(2,1)}, f32[8,512,512]{1,2,0:T(8,128)}, /*index=5*/bf16[8,512,512]{2,1,0:T(8,128)(2,1)}, s32[]{:T(128)}) while((s32[]{:T(128)}, bf16[512,512]{0,1:T(8,128)(2,1)}, f32[8,512,512]{1,2,0:T(8,128)}, ...), condition=%wide.region_1.2_spmd, body=%wide.region_0.1_spmd.sunk | while | flops 806617088 | bytes 17302612 | solution.py:62
  33.6 2.7 fusion.131
  41.8 2.7 fusion.131
  50.0 2.7 fusion.131
  58.1 2.7 fusion.131
  66.3 2.7 fusion.131
  74.5 2.7 fusion.131
  82.6 2.7 fusion.131
  90.8 2.7 fusion.131
  95.0 4.3 broadcast.158.clone.1
  99.3 67.7 %while.68 = (s32[]{:T(128)}, bf16[512,512]{0,1:T(8,128)(2,1)}, f32[8,512,512]{1,2,0:T(8,128)}, f32[8,512,512]{1,2,0:T(8,128)}, bf16[8,2,512,512]{3,2,1,0:T(8,128...) while((s32[]{:T(128)}, bf16[512,512]{0,1:T(8,128)(2,1)}, ...), condition=%wide.region_3.4_spmd.clone, body=%wide.region_2.3_spmd.clone.sunk | while | flops 807403520 | bytes 15204483 | solution.py:69
  103.0 2.5 fusion.140
  120.0 2.4 fusion.140
  136.9 2.4 fusion.140
  173.9 22.7 %collective-permute-done = f32[512,512]{0,1:T(8,128)S(1)} collective-permute-done((f32[512,512]{0,1:T(8,128)S(1)}, f32[512,512]{0,1:T(8,128)S(1)}, u32[]{:S(2)}, u32[]{:S(2)}) %collective-permute-start) | collective-permute-done | bytes 1048608 | tf_op jit(solution)/shard_map/ppermute | solution.py:13
  197.8 2.5 convolution_bitcast_fusion.4
  200.3 7.2 %collective-permute-start.1 = (f32[512,512]{0,1:T(8,128)}, f32[512,512]{0,1:T(8,128)}, u32[]{:S(2)}, u32[]{:S(2)}) collective-permute-start(f32[512,512]{0,1:T(8,128)} %convolution_bitcast_fusion.4), channel_id=1, source_target_pairs={{0,1},{1,2},{2,3},{3,4},{4,5},{5,6},{6,7},{7,8},{8,9},{9,10},{10,1... | collective-permute-start | bytes 3145736 | tf_op jit(solution)/shard_map/ppermute | solution.py:13
  213.9 13.3 %collective-permute-done.1 = f32[512,512]{0,1:T(8,128)} collective-permute-done((f32[512,512]{0,1:T(8,128)}, f32[512,512]{0,1:T(8,128)}, u32[]{:S(2)}, u32[]{:S(2)}) %collective-permute-start.1) | collective-permute-done | bytes 1048608 | tf_op jit(solution)/shard_map/ppermute | solution.py:13
  229.5 2.9 fusion.52
  232.4 4.3 broadcast.158.clone
  237.6 65.4 %while.66 = (s32[]{:T(128)}, bf16[512,512]{0,1:T(8,128)(2,1)}, f32[8,512,512]{1,2,0:T(8,128)}, bf16[8,2,512,512]{3,2,1,0:T(8,128)(2,1)}, f32[8,512,512]{1,2,0:T(8,128)}, /*index=5*/bf16[8,512,512]{2,1,0:T(8,128)(2,1)}, s32[]{:T(128)}) while((s32[]{:T(128)}, bf16[512,512]{0,1:T(8,128)(2,1)}, f32[8,512,512]{1,2,0:T(8,128)}, ...), condition=%wide.region_5.6_spmd, body=%wide.region_4.5_spmd.sunk | while | flops 806617088 | bytes 17302612 | solution.py:62
  241.5 2.7 fusion.135
  249.7 2.7 fusion.135
  257.8 2.7 fusion.135
  266.0 2.7 fusion.135
  274.2 2.7 fusion.135
  282.5 2.7 fusion.135
  290.6 2.7 fusion.135
  298.8 2.7 fusion.135
  303.0 4.3 broadcast.158
  307.4 67.7 %while.69 = (s32[]{:T(128)}, bf16[512,512]{0,1:T(8,128)(2,1)}, f32[8,512,512]{1,2,0:T(8,128)}, f32[8,512,512]{1,2,0:T(8,128)}, bf16[8,2,512,512]{3,2,1,0:T(8,128...) while((s32[]{:T(128)}, bf16[512,512]{0,1:T(8,128)(2,1)}, ...), condition=%wide.region_7.8_spmd.clone, body=%wide.region_6.7_spmd.clone.sunk | while | flops 807403520 | bytes 15204483 | solution.py:69
  311.1 2.5 fusion.144
  328.0 2.4 fusion.144
  375.0 9.9 %subtract_bitcast_fusion = (f32[1,8,512,256]{2,3,1,0:T(8,128)}, f32[1,8,512,256]{2,3,1,0:T(8,128)}) fusion(f32[8,512,512]{1,2,0:T(8,128)} %get-tuple-element.338, f32[]{:T(128)S(6)} %add.169, f32[]{:T(128)S(6)} %sub.71, f32[]{:T(128)} %bitcast.8, bf16[1,8,512,256]{2,3,1,0:T(8,128)(2,1)} %copy-done.2, f32[]{:T(128)} %bitcast.27), kind=kLoop, calls=%fused_computation.61 | loop fusion | flops 9437184 | bytes 18874384 | tf_op jit(solution)/shard_map/broadcast_in_dim | solution.py:110
  386.0 51.5 %reduce-scatter.3.cloned.1.call-done = f32[1,2,512,256]{2,3,1,0:T(8,128)} async-done(((f32[1,8,512,256]{2,3,1,0:T(8,128)}), f32[1,2,512,256]{2,3,1,0:T(8,128)}) %reduce-scatter.3.cloned.1.call-update) | async-done | bytes 1048592 | tf_op jit(solution)/shard_map/reduce_scatter | solution.py:109
  437.4 3.4 convolution_bitcast_fusion.6
  440.8 45.5 %reduce-scatter.5.cloned.1.call-done = f32[1,2,512,256]{2,3,1,0:T(8,128)} async-done(((f32[1,8,512,256]{2,3,1,0:T(8,128)}), f32[1,2,512,256]{2,3,1,0:T(8,128)}) %reduce-scatter.5.cloned.1.call-update) | async-done | bytes 1048592 | tf_op jit(solution)/shard_map/reduce_scatter | solution.py:110
  486.3 3.3 convolution_bitcast_fusion.5
  490.0 148.1 %all-reduce.5.cloned.1.call-done = (f32[256,256]{0,1:T(8,128)}, f32[256,256]{0,1:T(8,128)}) async-done(((f32[256,256]{0,1:T(8,128)}, f32[256,256]{0,1:T(8,128)}), (f32[256,256]{0,1:T(8,128)}, f32[256,256]{0,1:T(8,128)})) %all-reduce.5.cloned.1.call-update) | async-done | bytes 524304 | tf_op jit(solution)/shard_map/psum | solution.py:115
  640.3 11.7 %cholesky.50 = f32[128,128]{1,0:T(8,128)S(1)} custom-call(f32[128,128]{1,0:T(8,128)S(1)} %cholesky.118), custom_call_target="Cholesky" | custom-call | tf_op jit(solution)/shard_map/jit(cholesky)/cholesky | solution.py:119
  652.1 9.8 %custom-call.17 = f32[1,128,128]{1,2,0:T(8,128)S(1)} custom-call(f32[1,128,128]{2,1,0:T(8,128)S(1)} %get-tuple-element.519), custom_call_target="InvertDiagBlocksLowerTriangular" | custom-call | tf_op jit(solution)/shard_map/jit(cholesky)/cholesky | solution.py:119
  662.4 11.9 %cholesky.105 = f32[128,128]{1,0:T(8,128)S(1)} custom-call(f32[128,128]{1,0:T(8,128)S(1)} %convolution_subtract_fusion.3), custom_call_target="Cholesky" | custom-call | tf_op jit(solution)/shard_map/jit(cholesky)/cholesky | solution.py:119
  677.0 4.0 while.67
  681.0 19.7 %custom-call.18 = f32[2,128,128]{1,2,0:T(8,128)S(1)} custom-call(f32[2,128,128]{2,1,0:T(8,128)S(1)} %get-tuple-element.354), custom_call_target="InvertDiagBlocksLowerTriangular" | custom-call | tf_op jit(solution)/shard_map/triangular_solve | solution.py:17
  (228 shorter events, 246.0 us)
Async XLA Ops:
  7.2 430.3 %reduce-scatter.3.cloned.1.call-start = ((), (), s32[]{:S(2)}) async-start(), calls=%async_computation.2 | async-start | bytes 5242880 | tf_op jit(solution)/shard_map/reduce_scatter | solution.py:109
  15.4 6.9 copy-start.2
  15.9 2.1 copy-start
  18.0 4.2 copy-start.3
  168.3 28.2 %collective-permute-start = (f32[512,512]{0,1:T(8,128)S(1)}, f32[512,512]{0,1:T(8,128)S(1)}, u32[]{:S(2)}, u32[]{:S(2)}) collective-permute-start(f32[512,512]{0,1:T(8,128)S(1)} %slice_bitcast_fusion.1), channel_id=1, source_target_pairs={{1,0},{2,1},{3,2},{4,3},{5,4},{6,5},{7,6},{8,7},{9,8},{10,9},{11,1... | collective-permute-start | bytes 3145736 | tf_op jit(solution)/shard_map/ppermute | solution.py:13
  197.3 10.2 %copy-start.5 = (f32[1,4]{1,0:T(1,128)S(1)}, f32[1,4]{1,0:T(1,128)}, u32[]{:S(2)}) copy-start(f32[1,4]{1,0:T(1,128)} %param.23) | copy-start | bytes 52
  200.3 26.9 %collective-permute-start.1 = (f32[512,512]{0,1:T(8,128)}, f32[512,512]{0,1:T(8,128)}, u32[]{:S(2)}, u32[]{:S(2)}) collective-permute-start(f32[512,512]{0,1:T(8,128)} %convolution_bitcast_fusion.4), channel_id=1, source_target_pairs={{0,1},{1,2},{2,3},{3,4},{4,5},{5,6},{6,7},{7,8},{8,9},{9,10},{10,1... | collective-permute-start | bytes 3145736 | tf_op jit(solution)/shard_map/ppermute | solution.py:13
  212.9 14.2 %copy-start.1 = (f32[8,512,256]{1,2,0:T(8,128)S(1)}, f32[8,512,256]{1,2,0:T(8,128)}, u32[]{:S(2)}) copy-start(f32[8,512,256]{1,2,0:T(8,128)} %copy-done) | copy-start | bytes 12582916
  385.0 101.3 %reduce-scatter.5.cloned.1.call-start = ((), (), s32[]{:S(2)}) async-start(), calls=%async_computation.3 | async-start | bytes 5242880 | tf_op jit(solution)/shard_map/reduce_scatter | solution.py:110
  385.8 252.4 %all-reduce.5.cloned.1.call-start = ((), (), s32[]{:S(2)}) async-start(), calls=%async_computation.4 | async-start | bytes 1048576 | tf_op jit(solution)/shard_map/psum | solution.py:115
  437.4 52.2 %copy-start.4 = (f32[1,2,512,256]{2,3,1,0:T(8,128)S(1)}, f32[1,2,512,256]{2,3,1,0:T(8,128)}, u32[]{:S(2)}) copy-start(f32[1,2,512,256]{2,3,1,0:T(8,128)} %reduce-scatter.3.cloned.1.call-done) | copy-start | bytes 3145732
Sparse Core Ops, SparseCore 0:
  385.1 52.2 reduce-scatter.2
  440.0 46.3 reduce-scatter.4
  491.8 146.2 all-reduce.4
where the time goes:
time: 726 us; the launch traced here: 714 us
  waiting for transfers between devices  282 us (39%)
  other arithmetic  176 us (24%)
  local copies, waits for them, and re-layouts  127 us (17%)
  matrix products  99.8 us (14%)
  between operations  20.4 us (3%)
  starting transfers between devices  8.82 us (1%)
    psum x1, waiting for transfers between devices, on_device(): lax.psum((gram_part, projected_part), ('pole', 'dom'))  148 us
    dot_general x35, matrix products, complex_product(): jnp.dot(stacked, vectors.astype(jnp.bfloat16), preferred_element_type=jnp...  83.1 us
    dynamic_slice x64, local copies, waits for them, and re-layouts, partition_solve(): lax.scan(forward_step, initial, (inverse, source, previous))  82.9 us
    dynamic_update_slice x32, other arithmetic, partition_solve(): lax.scan(forward_step, initial, (inverse, source, previous))  60.9 us
    reduce_scatter x1, waiting for transfers between devices, on_device(): lax.psum_scatter(filtered_term[None], 'pole', scatter_dimension=1, tiled=...  51.5 us
    reduce_scatter x1, waiting for transfers between devices, on_device(): lax.psum_scatter(shifted_term[None], 'pole', scatter_dimension=1, tiled=T...  45.5 us
    ppermute x2, waiting for transfers between devices, shifted(): return lax.ppermute(x, axis, pairs)  36 us
    add x16, other arithmetic, backward_step(): partial_value + complex_product(block_inverse, real_product(couple_next,...  35.2 us
  transfers between devices with their start and end apart: 5, of which 5 were waited for; matrix products, arithmetic and copies ran while one was open for 1% of the time, Pallas kernels for 0%

commit v1 on v0

--- a/solution.py
+++ b/solution.py
@@ -112,7 +112,11 @@
     own_rows = owned[0].reshape(count * B, M)
     gram_part = inner_products(own_rows, own_rows)
     projected_part = inner_products(own_rows, shifted_owned[0].reshape(count * B, M))
-    gram_total, projected_total = lax.psum((gram_part, projected_part), ("pole", "dom"))
+
+    def _serve_plane(block_here):
+        return lax.psum(lax.psum(block_here, "pole"), axis_name="dom")
+
+    gram_total, projected_total = _serve_plane((gram_part, projected_part))
     row_total = blocks * B * lax.axis_size("dom")
     gram = gram_total / row_total
     projected = projected_total / row_total

time: 726 us -> 969 us (1.33)
  the two profiles are of different devices: /device:TPU:1 before, /device:TPU:0 now
where the time goes in v1:
time: 969 us; the launch traced here: 957 us
  waiting for transfers between devices  524 us (54%)
  other arithmetic  176 us (18%)
  local copies, waits for them, and re-layouts  127 us (13%)
  matrix products  99.8 us (10%)
  between operations  20.6 us (2%)
    psum x2, waiting for transfers between devices, _serve_plane(): return lax.psum(lax.psum(block_here, 'pole'), axis_name='dom')  392 us
    dot_general x35, matrix products, complex_product(): jnp.dot(stacked, vectors.astype(jnp.bfloat16), preferred_element_type=jnp...  83.1 us
    dynamic_slice x64, local copies, waits for them, and re-layouts, partition_solve(): lax.scan(forward_step, initial, (inverse, source, previous))  82.9 us
    dynamic_update_slice x32, other arithmetic, partition_solve(): lax.scan(forward_step, initial, (inverse, source, previous))  60.9 us
    reduce_scatter x1, waiting for transfers between devices, on_device(): lax.psum_scatter(filtered_term[None], 'pole', scatter_dimension=1, tiled=...  49.6 us
    reduce_scatter x1, waiting for transfers between devices, on_device(): lax.psum_scatter(shifted_term[None], 'pole', scatter_dimension=1, tiled=T...  45.5 us
    ppermute x2, waiting for transfers between devices, shifted(): return lax.ppermute(x, axis, pairs)  36.5 us
    add x16, other arithmetic, backward_step(): partial_value + complex_product(block_inverse, real_product(couple_next,...  35.4 us
  transfers between devices with their start and end apart: 6, of which 6 were waited for; matrix products, arithmetic and copies ran while one was open for 1% of the time, Pallas kernels for 0%

profile of v1, /device:TPU:0, one launch (start us, length us, event | category | flops | bytes accessed | tf_op | source)
XLA Modules:
  0.0 957.3 jit_solution(17405702631842131179)
XLA Ops:
  7.2 4.2 slice_bitcast_fusion
  12.5 2.9 copy.17
  18.0 4.2 concatenate.76
  24.6 4.3 broadcast.158.clone.2
  29.8 65.2 %while.65 = (s32[]{:T(128)}, bf16[512,512]{0,1:T(8,128)(2,1)}, f32[8,512,512]{1,2,0:T(8,128)}, bf16[8,2,512,512]{3,2,1,0:T(8,128)(2,1)}, f32[8,512,512]{1,2,0:T(8,128)}, /*index=5*/bf16[8,512,512]{2,1,0:T(8,128)(2,1)}, s32[]{:T(128)}) while((s32[]{:T(128)}, bf16[512,512]{0,1:T(8,128)(2,1)}, f32[8,512,512]{1,2,0:T(8,128)}, ...), condition=%wide.region_1.2_spmd, body=%wide.region_0.1_spmd.sunk | while | flops 806617088 | bytes 17302612 | solution.py:62
  33.7 2.7 fusion.131
  41.8 2.7 fusion.131
  49.9 2.7 fusion.131
  58.1 2.7 fusion.131
  66.3 2.7 fusion.131
  74.5 2.7 fusion.131
  82.6 2.7 fusion.131
  90.8 2.7 fusion.131
  95.0 4.3 broadcast.158.clone.1
  99.3 67.8 %while.68 = (s32[]{:T(128)}, bf16[512,512]{0,1:T(8,128)(2,1)}, f32[8,512,512]{1,2,0:T(8,128)}, f32[8,512,512]{1,2,0:T(8,128)}, bf16[8,2,512,512]{3,2,1,0:T(8,128...) while((s32[]{:T(128)}, bf16[512,512]{0,1:T(8,128)(2,1)}, ...), condition=%wide.region_3.4_spmd.clone, body=%wide.region_2.3_spmd.clone.sunk | while | flops 807403520 | bytes 15204483 | solution.py:69
  103.0 2.5 fusion.140
  120.1 2.4 fusion.140
  174.0 22.8 %collective-permute-done = f32[512,512]{0,1:T(8,128)S(1)} collective-permute-done((f32[512,512]{0,1:T(8,128)S(1)}, f32[512,512]{0,1:T(8,128)S(1)}, u32[]{:S(2)}, u32[]{:S(2)}) %collective-permute-start) | collective-permute-done | bytes 1048608 | tf_op jit(solution)/shard_map/ppermute | solution.py:13
  198.0 2.5 convolution_bitcast_fusion.4
  200.5 7.5 collective-permute-start.1
  214.6 13.7 %collective-permute-done.1 = f32[512,512]{0,1:T(8,128)} collective-permute-done((f32[512,512]{0,1:T(8,128)}, f32[512,512]{0,1:T(8,128)}, u32[]{:S(2)}, u32[]{:S(2)}) %collective-permute-start.1) | collective-permute-done | bytes 1048608 | tf_op jit(solution)/shard_map/ppermute | solution.py:13
  230.7 2.9 fusion.52
  233.6 4.3 broadcast.158.clone
  238.8 65.5 %while.66 = (s32[]{:T(128)}, bf16[512,512]{0,1:T(8,128)(2,1)}, f32[8,512,512]{1,2,0:T(8,128)}, bf16[8,2,512,512]{3,2,1,0:T(8,128)(2,1)}, f32[8,512,512]{1,2,0:T(8,128)}, /*index=5*/bf16[8,512,512]{2,1,0:T(8,128)(2,1)}, s32[]{:T(128)}) while((s32[]{:T(128)}, bf16[512,512]{0,1:T(8,128)(2,1)}, f32[8,512,512]{1,2,0:T(8,128)}, ...), condition=%wide.region_5.6_spmd, body=%wide.region_4.5_spmd.sunk | while | flops 806617088 | bytes 17302612 | solution.py:62
  242.7 2.7 fusion.135
  250.8 2.7 fusion.135
  259.0 2.7 fusion.135
  267.1 2.7 fusion.135
  275.4 2.7 fusion.135
  283.7 2.7 fusion.135
  291.8 2.7 fusion.135
  300.0 2.7 fusion.135
  304.3 4.3 broadcast.158
  308.6 67.7 %while.69 = (s32[]{:T(128)}, bf16[512,512]{0,1:T(8,128)(2,1)}, f32[8,512,512]{1,2,0:T(8,128)}, f32[8,512,512]{1,2,0:T(8,128)}, bf16[8,2,512,512]{3,2,1,0:T(8,128...) while((s32[]{:T(128)}, bf16[512,512]{0,1:T(8,128)(2,1)}, ...), condition=%wide.region_7.8_spmd.clone, body=%wide.region_6.7_spmd.clone.sunk | while | flops 807403520 | bytes 15204483 | solution.py:69
  312.3 2.5 fusion.144
  371.7 2.4 fusion.144
  376.3 10.0 %subtract_bitcast_fusion = (f32[1,8,512,256]{2,3,1,0:T(8,128)}, f32[1,8,512,256]{2,3,1,0:T(8,128)}) fusion(f32[8,512,512]{1,2,0:T(8,128)} %get-tuple-element.338, f32[]{:T(128)S(6)} %add.173, f32[]{:T(128)S(6)} %sub.71, f32[]{:T(128)} %bitcast.8, bf16[1,8,512,256]{2,3,1,0:T(8,128)(2,1)} %copy-done.2, f32[]{:T(128)} %bitcast.27), kind=kLoop, calls=%fused_computation.61 | loop fusion | flops 9437184 | bytes 18874384 | tf_op jit(solution)/shard_map/broadcast_in_dim | solution.py:110
  387.1 49.6 %reduce-scatter.3.cloned.1.call-done = f32[1,2,512,256]{2,3,1,0:T(8,128)} async-done(((f32[1,8,512,256]{2,3,1,0:T(8,128)}), f32[1,2,512,256]{2,3,1,0:T(8,128)}) %reduce-scatter.3.cloned.1.call-update) | async-done | bytes 1048592 | tf_op jit(solution)/shard_map/reduce_scatter | solution.py:109
  436.7 3.4 convolution_bitcast_fusion.6
  440.1 45.5 %reduce-scatter.5.cloned.1.call-done = f32[1,2,512,256]{2,3,1,0:T(8,128)} async-done(((f32[1,8,512,256]{2,3,1,0:T(8,128)}), f32[1,2,512,256]{2,3,1,0:T(8,128)}) %reduce-scatter.5.cloned.1.call-update) | async-done | bytes 1048592 | tf_op jit(solution)/shard_map/reduce_scatter | solution.py:110
  485.6 3.3 convolution_bitcast_fusion.5
  489.1 38.5 %all-reduce.9.cloned.1.call-done = (f32[256,256]{0,1:T(8,128)}, f32[256,256]{0,1:T(8,128)}) async-done(((f32[256,256]{0,1:T(8,128)}, f32[256,256]{0,1:T(8,128)}), (f32[256,256]{0,1:T(8,128)}, f32[256,256]{0,1:T(8,128)})) %all-reduce.9.cloned.1.call-update) | async-done | bytes 524304 | tf_op jit(solution)/shard_map/psum | solution.py:117
  528.0 353.3 %all-reduce.7.cloned.1.call-done = (f32[256,256]{0,1:T(8,128)}, f32[256,256]{0,1:T(8,128)}) async-done(((f32[256,256]{0,1:T(8,128)}, f32[256,256]{0,1:T(8,128)}), (f32[256,256]{0,1:T(8,128)}, f32[256,256]{0,1:T(8,128)})) %all-reduce.7.cloned.1.call-update) | async-done | bytes 524304 | tf_op jit(solution)/shard_map/psum | solution.py:117
  883.5 11.7 %cholesky.50 = f32[128,128]{1,0:T(8,128)S(1)} custom-call(f32[128,128]{1,0:T(8,128)S(1)} %cholesky.118), custom_call_target="Cholesky" | custom-call | tf_op jit(solution)/shard_map/jit(cholesky)/cholesky | solution.py:123
  895.2 9.8 %custom-call.17 = f32[1,128,128]{1,2,0:T(8,128)S(1)} custom-call(f32[1,128,128]{2,1,0:T(8,128)S(1)} %get-tuple-element.521), custom_call_target="InvertDiagBlocksLowerTriangular" | custom-call | tf_op jit(solution)/shard_map/jit(cholesky)/cholesky | solution.py:123
  905.5 11.7 %cholesky.105 = f32[128,128]{1,0:T(8,128)S(1)} custom-call(f32[128,128]{1,0:T(8,128)S(1)} %convolution_subtract_fusion.3), custom_call_target="Cholesky" | custom-call | tf_op jit(solution)/shard_map/jit(cholesky)/cholesky | solution.py:123
  920.0 4.2 while.67
  924.2 19.7 %custom-call.18 = f32[2,128,128]{1,2,0:T(8,128)S(1)} custom-call(f32[2,128,128]{2,1,0:T(8,128)S(1)} %get-tuple-element.354), custom_call_target="InvertDiagBlocksLowerTriangular" | custom-call | tf_op jit(solution)/shard_map/triangular_solve | solution.py:17
  (231 shorter events, 248.8 us)
Async XLA Ops:
  7.2 429.5 %reduce-scatter.3.cloned.1.call-start = ((), (), s32[]{:S(2)}) async-start(), calls=%async_computation.2 | async-start | bytes 5242880 | tf_op jit(solution)/shard_map/reduce_scatter | solution.py:109
  15.4 6.9 copy-start.2
  16.0 2.1 copy-start
  18.0 4.3 copy-start.3
  168.4 28.3 %collective-permute-start = (f32[512,512]{0,1:T(8,128)S(1)}, f32[512,512]{0,1:T(8,128)S(1)}, u32[]{:S(2)}, u32[]{:S(2)}) collective-permute-start(f32[512,512]{0,1:T(8,128)S(1)} %slice_bitcast_fusion.1), channel_id=1, source_target_pairs={{1,0},{2,1},{3,2},{4,3},{5,4},{6,5},{7,6},{8,7},{9,8},{10,9},{11,1... | collective-permute-start | bytes 3145736 | tf_op jit(solution)/shard_map/ppermute | solution.py:13
  197.5 10.5 %copy-start.5 = (f32[1,4]{1,0:T(1,128)S(1)}, f32[1,4]{1,0:T(1,128)}, u32[]{:S(2)}) copy-start(f32[1,4]{1,0:T(1,128)} %param.23) | copy-start | bytes 52
  200.5 27.8 %collective-permute-start.1 = (f32[512,512]{0,1:T(8,128)}, f32[512,512]{0,1:T(8,128)}, u32[]{:S(2)}, u32[]{:S(2)}) collective-permute-start(f32[512,512]{0,1:T(8,128)} %convolution_bitcast_fusion.4), channel_id=1, source_target_pairs={{0,1},{1,2},{2,3},{3,4},{4,5},{5,6},{6,7},{7,8},{8,9},{9,10},{10,1... | collective-permute-start | bytes 3145736 | tf_op jit(solution)/shard_map/ppermute | solution.py:13
  213.6 14.7 %copy-start.1 = (f32[8,512,256]{1,2,0:T(8,128)S(1)}, f32[8,512,256]{1,2,0:T(8,128)}, u32[]{:S(2)}) copy-start(f32[8,512,256]{1,2,0:T(8,128)} %copy-done) | copy-start | bytes 12582916
  386.3 99.3 %reduce-scatter.5.cloned.1.call-start = ((), (), s32[]{:S(2)}) async-start(), calls=%async_computation.3 | async-start | bytes 5242880 | tf_op jit(solution)/shard_map/reduce_scatter | solution.py:110
  387.1 140.5 %all-reduce.9.cloned.1.call-start = ((), (), s32[]{:S(2)}) async-start(), calls=%async_computation.5 | async-start | bytes 1048576 | tf_op jit(solution)/shard_map/psum | solution.py:117
  436.7 90.9 %copy-start.4 = (f32[1,2,512,256]{2,3,1,0:T(8,128)S(1)}, f32[1,2,512,256]{2,3,1,0:T(8,128)}, u32[]{:S(2)}) copy-start(f32[1,2,512,256]{2,3,1,0:T(8,128)} %reduce-scatter.3.cloned.1.call-done) | copy-start | bytes 3145732
  488.9 392.4 %all-reduce.7.cloned.1.call-start = ((), (), s32[]{:S(2)}) async-start(), calls=%async_computation.4 | async-start | bytes 1048576 | tf_op jit(solution)/shard_map/psum | solution.py:117
Sparse Core Ops, SparseCore 0:
  386.5 50.2 reduce-scatter.2
  439.2 46.3 reduce-scatter.4
  489.0 38.5 all-reduce.8
  530.0 351.2 all-reduce.6
